TPU v7x, 32 devices: a whole 2x2x4 slice. The times are simulated.
32 devices in a mesh: rows: 8 (over y, x, core), cols: 4 (over z).
Axes of the slice: x: 2, y: 2, z: 4, core: 2. Of those that a mesh axis runs over, the one named last changes fastest.
Arguments:
- sheet: bfloat16 [8, 1024, 1024], P('cols', 'rows'), may hold values from -600 to 600
- w_in: bfloat16 [1024, 16, 384], P(None, 'cols'), may hold values from -0.1875 to 0.1875
- w_out: bfloat16 [16, 128, 1024], P('cols'), may hold values from -0.125 to 0.125
Outputs:
- mixed: bfloat16 [8, 1024, 1024], P('cols', 'rows')
All inputs are finite; a program needn't handle non-finite values.
Results may differ from a plain program's by a relative error of at most 0.0067.
Values may be sent and summed in bfloat16 or wider, within the bound.
A program may use at most 128 MiB of HBM per device.

v0:
```python
import jax
import jax.numpy as jnp
from jax import lax
from jax.sharding import PartitionSpec as P


def prefix(x, axis, combine, identity):
    peers, mine = (lax.axis_size(axis), lax.axis_index(axis))
    everything = lax.all_gather(x, axis)
    start = jnp.broadcast_to(jnp.asarray(identity, x.dtype), x.shape)

    def turn(k, before):
        reached = k < mine
        new = combine(before, everything[k])
        return jnp.where(reached, new, before)

    return lax.fori_loop(0, peers, turn, start)


def head_norm(values):
    return values * lax.rsqrt(jnp.mean(values * values, axis=-1, keepdims=True) + 1e-06)


def feature_map(values):
    return jax.nn.elu(values) + 1.0


def finish_proj(proj):
    parts = [
        head_norm(proj[..., 0, :]),
        head_norm(proj[..., 1, :]),
        proj[..., 2, :],
        feature_map(proj[..., 3, :]),
        feature_map(proj[..., 4, :]),
        proj[..., 5, :],
    ]
    return jnp.stack(parts, axis=-2).astype(jnp.bfloat16)


def add_states(earlier, later):
    return earlier + later


def body(sheet, w_in, w_out):
    high = lax.Precision.HIGHEST
    width = sheet.shape[2]
    heads_here = w_in.shape[1]
    hdim = w_out.shape[1] // 2
    w_flat = w_in.reshape(width, heads_here * 6 * hdim)
    piece = lax.all_gather(sheet, "cols", axis=0, tiled=True)
    xfull = piece.astype(jnp.float32)
    normed = (xfull * lax.rsqrt(jnp.mean(xfull * xfull, axis=-1, keepdims=True) + 1e-06)).astype(
        jnp.bfloat16
    )
    proj = jnp.dot(normed.reshape(-1, width), w_flat, preferred_element_type=jnp.float32)
    proj = proj.reshape(piece.shape[0], piece.shape[1], heads_here, 6, hdim)
    projected = finish_proj(proj).reshape(piece.shape[0], piece.shape[1], heads_here * 6 * hdim)
    all_cols = projected.shape[0]
    row_count = projected.shape[1]
    parts = projected.reshape(all_cols, row_count, heads_here, 6, hdim)
    qrow, krow, vrow = (parts[:, :, :, 0], parts[:, :, :, 1], parts[:, :, :, 2])
    fq, fk, vcol = (parts[:, :, :, 3], parts[:, :, :, 4], parts[:, :, :, 5])
    scale = hdim ** (-0.5)
    score = jnp.einsum("crhd,erhd->rhce", qrow, krow, preferred_element_type=jnp.float32) * scale
    expo = jnp.exp(score)
    weights = (expo / jnp.sum(expo, axis=-1, keepdims=True)).astype(jnp.bfloat16)
    orow = jnp.einsum("rhce,erhd->crhd", weights, vrow, preferred_element_type=jnp.float32).astype(
        jnp.bfloat16
    )
    states = jnp.einsum("crhk,crhv->chkv", fk, vcol, preferred_element_type=jnp.float32)
    prior = prefix(states, "rows", add_states, jnp.zeros_like(states))
    causal = (jnp.arange(row_count)[:, None] >= jnp.arange(row_count)[None, :]).astype(jnp.float32)
    inner = jnp.einsum("cthd,cshd->chts", fq, fk, preferred_element_type=jnp.float32) * causal
    local = jnp.einsum("chts,cshv->cthv", inner, vcol.astype(jnp.float32), precision=high)
    carried = jnp.einsum("cthk,chkv->cthv", fq.astype(jnp.float32), prior, precision=high)
    ocol = head_norm(carried + local).astype(jnp.bfloat16)
    results = jnp.stack([orow, ocol], axis=3).reshape(all_cols, row_count, heads_here * 2 * hdim)
    w_local = w_out.reshape(heads_here * 2 * hdim, width)
    own_cols = all_cols // lax.axis_size("cols")
    flat = jnp.dot(
        results.reshape(lax.axis_size("cols") * own_cols * row_count, -1),
        w_local,
        preferred_element_type=jnp.float32,
    )
    mixed = lax.psum_scatter(
        flat.reshape(lax.axis_size("cols") * own_cols, row_count, width),
        "cols",
        scatter_dimension=0,
        tiled=True,
    )
    return mixed.astype(jnp.bfloat16)


def solution(mesh):
    return jax.shard_map(
        body,
        mesh=mesh,
        in_specs=(P("cols", "rows", None), P(None, "cols", None), P("cols", None, None)),
        out_specs=P("cols", "rows", None),
        check_vma=False,
    )
```

profile of v0, /device:TPU:0, one launch (start us, length us, event | category | flops | bytes accessed | tf_op | source)
XLA Modules:
  0.0 232.4 jit_solution(18211246727219181485)
XLA Ops:
  6.5 0.0 copy-start
  6.5 0.0 all-gather.4.cloned.1.call-start
  6.5 0.7 all-gather.4.cloned.1.call-update
  7.3 0.0 all-gather.6.cloned.1.call-start
  7.3 4.1 %copy.70 = bf16[128,8,4,384]{3,1,2,0:T(8,128)(2,1)} copy(bf16[128,8,4,384]{3,2,1,0:T(4,128)(2,1)} %bitcast.64) | data formatting | bytes 6291456
  11.4 4.6 %copy.48 = bf16[1536,1024]{1,0:T(8,128)(2,1)} copy(bf16[1536,1024]{0,1:T(8,128)(2,1)} %bitcast.61) | data formatting | bytes 6291456 | tf_op jit(solution)/shard_map/dot_general | solution.py:55
  16.1 41.5 %all-gather.4.cloned.1.call-done = bf16[8,128,1024]{2,1,0:T(8,128)(2,1)} async-done(((bf16[2,128,1024]{2,1,0:T(8,128)(2,1)}), bf16[8,128,1024]{2,1,0:T(8,128)(2,1)}) %all-gather.4.cloned.1.call-update) | async-done | bytes 2097168 | tf_op jit(solution)/shard_map/all_gather | solution.py:50
  57.6 2.1 fusion
  59.7 6.2 %fusion.41 = (bf16[8,128,4,6,64]{1,4,3,2,0:T(8,128)(2,1)S(1)}, f32[8,128,4,6,64]{1,4,3,2,0:T(8,128)S(1)}) fusion(bf16[4,6,64,1024,1]{3,2,1,0,4:T(8,128)(2,1)} %bitcast.65, bf16[8,128,1024]{2,1,0:T(8,128)(2,1)} %all-gather.4.cloned.1.call-done, f32[8,128]{1,0:T(8,128)S(1)} %add_rsqrt_fusion), kind=kOutput, calls=%fused_computation.56 | convolution fusion | flops 3225944064 | bytes 14684160 | tf_op jit(solution)/shard_map/dot_general | solution.py:55
  65.9 0.0 copy-start.1
  65.9 0.0 copy-start.3
  65.9 2.7 %copy-done.1 = f32[8,128,4,6,64]{1,4,3,2,0:T(8,128)} copy-done((f32[8,128,4,6,64]{1,4,3,2,0:T(8,128)}, f32[8,128,4,6,64]{1,4,3,2,0:T(8,128)S(1)}, u32[]{:S(2)}) %copy-start.1) | copy-done | bytes 6291480
  68.6 0.9 copy-done.3
  69.5 1.5 fusion.26
  71.0 0.0 all-gather.6.cloned.1.call-update
  71.0 0.2 reduce-scatter.2.cloned.1.call-start
  71.3 1.9 slice_bitcast_fusion.1
  73.2 2.5 %copy.56 = bf16[8,128,4,64]{3,0,2,1:T(8,128)(2,1)S(1)} copy(bf16[8,128,4,64]{1,3,2,0:T(8,128)(2,1)} %slice_bitcast_fusion.1) | data formatting | bytes 1048576 | tf_op jit(solution)/shard_map/squeeze | solution.py:61
  75.6 2.1 multiply_reduce_fusion.1
  77.8 3.0 %fusion.22 = (bf16[8,128,4,64]{1,3,2,0:T(8,128)(2,1)}, bf16[8,128,4,64]{1,3,2,0:T(8,128)(2,1)}) fusion(f32[8,128,4,6,64]{1,4,3,2,0:T(8,128)} %copy-done.1, f32[8,128,4]{1,2,0:T(4,128)S(1)} %copy.52, f32[8,128,4]{1,2,0:T(4,128)S(1)} %copy.50), kind=kLoop, calls=%fused_computation.31 | loop fusion | flops 1048576 | bytes 3178496 | tf_op jit(solution)/shard_map/squeeze | solution.py:61
  80.8 3.3 %copy.53 = bf16[8,128,4,64]{3,0,2,1:T(8,128)(2,1)} copy(bf16[8,128,4,64]{1,3,2,0:T(8,128)(2,1)} %get-tuple-element.111) | data formatting | bytes 1048576 | tf_op jit(solution)/shard_map/squeeze | solution.py:61
  84.1 3.4 %copy.54 = bf16[8,128,4,64]{3,0,2,1:T(8,128)(2,1)} copy(bf16[8,128,4,64]{1,3,2,0:T(8,128)(2,1)} %get-tuple-element.110) | data formatting | bytes 1048576 | tf_op jit(solution)/shard_map/squeeze | solution.py:61
  87.5 3.6 %fusion.42 = f32[128,4,8,8]{2,3,1,0:T(8,128)} fusion(bf16[8,128,4,64]{3,0,2,1:T(8,128)(2,1)} %copy.53, bf16[8,128,4,64]{3,0,2,1:T(8,128)(2,1)} %copy.54), kind=kOutput, calls=%fused_computation.57 | convolution fusion | flops 4194304 | bytes 1179648 | tf_op jit(solution)/shard_map/crhd,erhd->rhce/dot_general | solution.py:64
  91.0 2.7 %copy.55 = f32[128,4,8,8]{0,3,2,1:T(8,128)S(1)} copy(f32[128,4,8,8]{2,3,1,0:T(8,128)} %fusion.42) | data formatting | bytes 262144 | tf_op jit(solution)/shard_map/crhd,erhd->rhce/dot_general | solution.py:64
  93.8 2.4 %copy.57 = bf16[128,4,8,8]{3,2,1,0:T(8,128)(2,1)} copy(bf16[128,4,8,8]{0,3,2,1:T(8,128)(2,1)S(1)} %divide_convert_fusion) | data formatting | bytes 131072 | tf_op jit(solution)/shard_map/convert_element_type | solution.py:66
  96.2 2.9 %fusion.43 = bf16[128,4,64,8]{2,3,1,0:T(8,128)(2,1)} fusion(bf16[8,128,4,64]{3,0,2,1:T(8,128)(2,1)S(1)} %copy.56, bf16[128,4,8,8]{3,2,1,0:T(8,128)(2,1)} %copy.57), kind=kOutput, calls=%fused_computation.58 | convolution fusion | flops 4194304 | bytes 1114112 | tf_op jit(solution)/shard_map/rhce,erhd->crhd/dot_general | solution.py:67
  99.1 2.2 copy.58
  101.3 4.0 %fusion.35 = f32[8,4,128,128]{3,2,1,0:T(8,128)} fusion(f32[8,128,4,6,64]{1,4,3,2,0:T(8,128)} %copy-done.1), kind=kOutput, calls=%fused_computation.54 | convolution fusion | flops 69730304 | bytes 4194304 | tf_op jit(solution)/shard_map/cthd,cshd->chts/dot_general | solution.py:73
  105.2 19.1 %all-gather.6.cloned.1.call-done = f32[64,4,64,64]{3,2,1,0:T(8,128)} async-done(((f32[8,4,64,64]{3,2,1,0:T(8,128)}), f32[64,4,64,64]{3,2,1,0:T(8,128)}) %all-gather.6.cloned.1.call-update) | async-done | bytes 4194320 | tf_op jit(solution)/shard_map/all_gather | solution.py:9
  124.3 12.9 %while.14 = (s32[]{:T(128)}, f32[8,4,64,64]{3,2,1,0:T(8,128)S(1)}, s32[]{:T(128)}, f32[8,8,4,64,64]{4,3,2,1,0:T(8,128)}, s32[]{:T(128)}, /*index=5*/s32[]{:T(128)}) while((s32[]{:T(128)}, f32[8,4,64,64]{3,2,1,0:T(8,128)S(1)}, s32[]{:T(128)}, f32[8,8,4,64,64]{4,3,2,1,0:T(8,128)}, s32[]{:T(128)}, /*index=5*/s32[]{:T(128)}) %tuple.46), condition=%wide.region_5.6_spmd.clone, body=%wide.region_4.5_spmd.clone.sunk | while | flops 393220 | bytes 1572965 | solution.py:17
  124.3 1.6 add_select_fusion.2
  125.9 1.6 add_select_fusion.2
  127.5 1.6 add_select_fusion.2
  129.2 1.6 add_select_fusion.2
  130.8 1.6 add_select_fusion.2
  132.4 1.6 add_select_fusion.2
  134.0 1.6 add_select_fusion.2
  135.6 1.6 add_select_fusion.2
  137.2 0.0 copy-start.2
  137.2 2.7 %fusion.39 = f32[8,4,64,128]{3,2,1,0:T(8,128)S(1)} fusion(f32[8,4,64,64]{3,2,1,0:T(8,128)S(1)} %get-tuple-element.84, f32[8,128,4,6,64]{1,4,3,2,0:T(8,128)} %copy-done.1), kind=kOutput, calls=%fused_computation.55 | convolution fusion | flops 202637312 | bytes 2621440 | tf_op jit(solution)/shard_map/cthk,chkv->cthv/dot_general | solution.py:75
  139.9 0.0 copy-done.2
  139.9 3.3 %multiply_reduce_fusion = (f32[8,128,4]{1,2,0:T(4,128)S(1)}, f32[8,128,4,64]{1,3,2,0:T(8,128)S(1)}) fusion(f32[8,4,64,128]{3,2,1,0:T(8,128)S(1)} %fusion.39, f32[8,4,128,128]{3,2,1,0:T(8,128)S(1)} %copy-done.2, f32[128,128]{1,0:T(8,128)S(1)} %fusion.28, bf16[8,128,4,6,64]{1,4,3,2,0:T(8,128)(2,1)} %copy-done.3), kind=kOutput, calls=%fused_computation.24 | convolution fusion | flops 403959808 | bytes 4800512 | tf_op jit(solution)/shard_map/chts,cshv->cthv/dot_general | solution.py:74
  143.2 0.1 fusion.23
  143.4 0.1 pad_maximum_fusion
  143.5 0.1 copy.63
  143.6 0.0 copy-done
  143.6 3.2 %fusion.44 = f32[8,128,1024]{2,1,0:T(8,128)} fusion(bf16[8,128,512]{1,2,0:T(8,128)(2,1)S(1)} %bitcast.62, bf16[512,1024,1]{1,0,2:T(8,128)(2,1)S(1)} %bitcast.60), kind=kOutput, calls=%fused_computation.59 | convolution fusion | flops 1073741824 | bytes 6291456 | tf_op jit(solution)/shard_map/dot_general | solution.py:80
  146.8 0.0 reduce-scatter.2.cloned.1.call-update
  146.8 76.9 %reduce-scatter.2.cloned.1.call-done = f32[2,128,1024]{2,1,0:T(8,128)} async-done(((f32[8,128,1024]{2,1,0:T(8,128)}), f32[2,128,1024]{2,1,0:T(8,128)}) %reduce-scatter.2.cloned.1.call-update) | async-done | bytes 1048592 | tf_op jit(solution)/shard_map/reduce_scatter | solution.py:85
  223.8 2.1 convert_element_type.38
  (10 shorter events, 0.2 us)
Async XLA Ops:
  6.5 137.0 %copy-start = (bf16[4,128,1024]{2,1,0:T(8,128)(2,1)S(1)}, bf16[4,128,1024]{2,1,0:T(8,128)(2,1)}, u32[]{:S(2)}) copy-start(bf16[4,128,1024]{2,1,0:T(8,128)(2,1)} %param.7) | copy-start | bytes 3145732
  6.5 51.1 %all-gather.4.cloned.1.call-start = ((), (), s32[]{:S(2)}) async-start(), calls=%async_computation.1 | async-start | bytes 2621440 | tf_op jit(solution)/shard_map/all_gather | solution.py:50
  7.3 117.0 %all-gather.6.cloned.1.call-start = ((), (), s32[]{:S(2)}) async-start(), calls=%async_computation.3 | async-start | bytes 9437184 | tf_op jit(solution)/shard_map/all_gather | solution.py:9
  65.9 2.7 %copy-start.1 = (f32[8,128,4,6,64]{1,4,3,2,0:T(8,128)}, f32[8,128,4,6,64]{1,4,3,2,0:T(8,128)S(1)}, u32[]{:S(2)}) copy-start(f32[8,128,4,6,64]{1,4,3,2,0:T(8,128)S(1)} %get-tuple-element.113) | copy-start | bytes 18874372
  65.9 3.6 %copy-start.3 = (bf16[8,128,4,6,64]{1,4,3,2,0:T(8,128)(2,1)}, bf16[8,128,4,6,64]{1,4,3,2,0:T(8,128)(2,1)S(1)}, u32[]{:S(2)}) copy-start(bf16[8,128,4,6,64]{1,4,3,2,0:T(8,128)(2,1)S(1)} %get-tuple-element.112) | copy-start | bytes 9437188
  71.0 152.7 %reduce-scatter.2.cloned.1.call-start = ((), (), s32[]{:S(2)}) async-start(), calls=%async_computation.2 | async-start | bytes 5242880 | tf_op jit(solution)/shard_map/reduce_scatter | solution.py:85
  137.2 2.7 %copy-start.2 = (f32[8,4,128,128]{3,2,1,0:T(8,128)S(1)}, f32[8,4,128,128]{3,2,1,0:T(8,128)}, u32[]{:S(2)}) copy-start(f32[8,4,128,128]{3,2,1,0:T(8,128)} %fusion.35) | copy-start | bytes 6291460
Sparse Core Ops, SparseCore 0:
  8.9 48.6 all-gather.3
  71.2 53.0 all-gather.5
  147.0 76.7 reduce-scatter.1
where the time goes:
time: 233 us; the launch traced here: 232 us
  waiting for transfers between devices  138 us (59%)
  local copies, waits for them, and re-layouts  30.7 us (13%)
  matrix products  27.3 us (12%)
  other arithmetic  22.4 us (10%)
  between operations  13.3 us (6%)
    reduce_scatter x1, waiting for transfers between devices, body(): lax.psum_scatter(flat.reshape(lax.axis_size('cols') * own_cols, row_count...  76.9 us
    all_gather x1, waiting for transfers between devices, body(): piece = lax.all_gather(sheet, 'cols', axis=0, tiled=True)  41.5 us
    all_gather x1, waiting for transfers between devices, prefix(): everything = lax.all_gather(x, axis)  19.1 us
    select_n x8, other arithmetic, turn(): return jnp.where(reached, new, before)  12.7 us
    squeeze x4, local copies, waits for them, and re-layouts, body(): qrow, krow, vrow = (parts[:, :, :, 0], parts[:, :, :, 1], parts[:, :, :, 2])  11 us
    unnamed x9, local copies, waits for them, and re-layouts  7.73 us
    dot_general x1, matrix products, body(): jnp.dot(normed.reshape(-1, width), w_flat, preferred_element_type=jnp.flo...  6.19 us
  transfers between devices with their start and end apart: 3, of which 3 were waited for; matrix products, arithmetic and copies ran while one was open for 18% of the time, Pallas kernels for 0%

commit v1 on v0

v1 whole, which is shorter than its diff:
```python
import functools

import jax
import jax.numpy as jnp
from jax import lax
from jax.experimental import pallas as pl
from jax.experimental.pallas import tpu as pltpu
from jax.sharding import PartitionSpec as P

MESH = pl.DeviceIdType.MESH
F32, BF16 = jnp.float32, jnp.bfloat16
EPS = 1e-06
GROUP = 16


def dot(a, b, dims=((1,), (0,))):
    return lax.dot_general(a, b, (dims, ((), ())), preferred_element_type=F32)


def kernel(n, stages, x_ref, w_hbm, wo_hbm, out_ref, w, wo, buf, feat, tot, prior, st_send, st_recv, res, psend,
           precv, acc, load_sem, right_send, right_recv, left_send, left_recv, st_ssem, st_rsem, p_ssem, p_rsem):
    own, rows, width = x_ref.shape
    heads = w.shape[1] // 384
    hdim = 64
    c = lax.axis_index("cols")
    r = lax.axis_index("rows")

    w_copy = pltpu.make_async_copy(w_hbm, w, load_sem.at[0])
    wo_copy = pltpu.make_async_copy(wo_hbm, wo, load_sem.at[1])
    w_copy.start()
    wo_copy.start()

    both = jnp.minimum(c, n - 1 - c)
    more_left = c > n - 1 - c

    def place(s):
        paired = s <= 2 * both
        dist = jnp.where(paired, (s + 1) // 2, s - both)
        is_left = jnp.where(paired, s % 2 == 1, more_left)
        return dist, is_left, jnp.where(is_left, c - dist, c + dist)

    barrier = pltpu.get_barrier_semaphore()
    for s in range(1, n):
        pl.semaphore_signal(barrier, inc=1, device_id={"cols": lax.rem(c + s, n)}, device_id_type=MESH)
    for k in range(stages):
        pl.semaphore_signal(barrier, inc=1, device_id={"rows": partner(r, k)}, device_id_type=MESH)

    for i in range(own):
        xf = x_ref[i].astype(F32)
        buf[c, i] = (xf * lax.rsqrt(jnp.mean(xf * xf, axis=-1, keepdims=True) + EPS)).astype(BF16)
    pl.semaphore_wait(barrier, n - 1 + stages)

    def hop(shard, i, to_right):
        ssem, rsem = (right_send, right_recv) if to_right else (left_send, left_recv)
        to = jnp.minimum(c + 1, n - 1) if to_right else jnp.maximum(c - 1, 0)
        return pltpu.make_async_remote_copy(
            src_ref=buf.at[shard, i], dst_ref=buf.at[shard, i], send_sem=ssem.at[shard, i], recv_sem=rsem.at[shard, i],
            device_id={"cols": to}, device_id_type=MESH)

    for i in range(own):
        @pl.when(c < n - 1)
        def _():
            hop(c, i, True).start()

        @pl.when(c > 0)
        def _():
            hop(c, i, False).start()

    lane = lax.broadcasted_iota(jnp.int32, (1, 128), 1)
    low = lane < hdim
    spread = jnp.where(
        (lax.broadcasted_iota(jnp.int32, (128, 128), 0) < hdim) == (lax.broadcasted_iota(jnp.int32, (128, 128), 1) < hdim),
        1.0 / hdim, 0.0).astype(BF16)

    def phi(v):
        return jnp.where(v > 0, v + 1.0, jnp.exp(jnp.minimum(v, 0.0)))

    def project(s, shard):
        for i in range(own):
            xn = buf[shard, i]
            states = []
            for h in range(heads):
                proj = dot(xn, w[:, h * 384:(h + 1) * 384])
                t0, t1, t2 = proj[:, :128], proj[:, 128:256], proj[:, 256:]
                t0 = t0 * lax.rsqrt(dot((t0 * t0).astype(BF16), spread) + EPS)
                t1 = jnp.where(low, t1, phi(t1))
                t2 = jnp.where(low, phi(t2), t2).astype(BF16)
                feat[s, i, :, h * 384:h * 384 + 128] = t0.astype(BF16)
                feat[s, i, :, h * 384 + 128:h * 384 + 256] = t1.astype(BF16)
                feat[s, i, :, h * 384 + 256:h * 384 + 384] = t2
                states.append(dot(t2, t2, ((0,), (0,)))[:hdim, hdim:])
            tot[s, i] = jnp.concatenate(states, axis=-1)

    def exchange(s, k):
        return pltpu.make_async_remote_copy(
            src_ref=st_send.at[s, k], dst_ref=st_recv.at[s, k], send_sem=st_ssem.at[s, k], recv_sem=st_rsem.at[s, k],
            device_id={"rows": partner(r, k)}, device_id_type=MESH)

    def begin(s, k):
        st_send[s, k] = tot[s].astype(BF16)
        exchange(s, k).start()

    def advance(s, k):
        exchange(s, k).wait()
        got = st_recv[s, k].astype(F32)
        later = ((r // (1 << k)) % 2).astype(F32)
        prior[s] += got * later
        if k + 1 < stages:
            tot[s] += got
            begin(s, k + 1)

    prior[...] = jnp.zeros_like(prior)
    pending = []

    def tick():
        for at in list(pending):
            advance(*at)
            pending.remove(at)
            if at[1] + 1 < stages:
                pending.append((at[0], at[1] + 1))

    w_copy.wait()
    for s in range(n):
        dist, is_left, shard = place(s) if s else (0, None, c)
        if s:
            for i in range(own):
                @pl.when(is_left)
                def _():
                    hop(shard, i, True).wait_recv()

                    @pl.when(c < n - 1)
                    def _():
                        hop(shard, i, True).start()

                @pl.when(jnp.logical_not(is_left))
                def _():
                    hop(shard, i, False).wait_recv()

                    @pl.when(c > 0)
                    def _():
                        hop(shard, i, False).start()
        project(s, shard)
        begin(s, 0)
        tick()
        pending.append((s, 0))

    cells = n * own * GROUP
    same = (lax.broadcasted_iota(jnp.int32, (cells, cells), 0) % GROUP) == (
        lax.broadcasted_iota(jnp.int32, (cells, cells), 1) % GROUP)

    def row_group(g, carry):
        at = pl.ds(pl.multiple_of(g * GROUP, GROUP), GROUP)
        for h in range(heads):
            t0 = feat[:, :, at, h * 384:h * 384 + 128].reshape(cells, 128)
            v = feat[:, :, at, h * 384 + 128:h * 384 + 256].reshape(cells, 128)[:, :hdim]
            score = dot(t0[:, :hdim], t0[:, hdim:], ((1,), (1,))) * (hdim ** -0.5)
            expo = jnp.where(same, jnp.exp(score), 0.0)
            weights = (expo / jnp.sum(expo, axis=-1, keepdims=True)).astype(BF16)
            orow = dot(weights, v).astype(BF16)
            res[:, :, at, h * 128:h * 128 + hdim] = orow.reshape(n, own, GROUP, hdim)
        return carry

    groups = rows // GROUP
    cuts = [groups * p // stages for p in range(stages + 1)]
    for p in range(stages):
        lax.fori_loop(cuts[p], cuts[p + 1], row_group, 0)
        tick()
    while pending:
        tick()

    causal = lax.broadcasted_iota(jnp.int32, (rows, rows), 0) >= lax.broadcasted_iota(jnp.int32, (rows, rows), 1)

    def columns(s):
        for i in range(own):
            for h in range(heads):
                fq = feat[s, i, :, h * 384 + 128:h * 384 + 256][:, hdim:]
                t2 = feat[s, i, :, h * 384 + 256:h * 384 + 384]
                fk, vcol = t2[:, :hdim], t2[:, hdim:]
                inner = jnp.where(causal, dot(fq, fk, ((1,), (1,))), 0.0).astype(BF16)
                pre = dot(inner, vcol) + dot(fq, prior[s, i, :, h * hdim:(h + 1) * hdim].astype(BF16))
                ocol = pre * lax.rsqrt(jnp.mean(pre * pre, axis=-1, keepdims=True) + EPS)
                res[s, i, :, h * 128 + hdim:(h + 1) * 128] = ocol.astype(BF16)

    def partial(s, shard):
        return pltpu.make_async_remote_copy(
            src_ref=psend.at[s], dst_ref=precv.at[c], send_sem=p_ssem.at[s], recv_sem=p_rsem.at[c],
            device_id={"cols": shard}, device_id_type=MESH)

    wo_copy.wait()
    for s in list(range(n - 1, 0, -1)) + [0]:
        columns(s)
        for i in range(own):
            part = dot(res[s, i], wo[...])
            if s:
                psend[s, i] = part.astype(BF16)
            else:
                acc[i] = part
        if s:
            partial(s, place(s)[2]).start()

    for s in range(1, n):
        shard = place(s)[2]
        pltpu.make_async_remote_copy(
            src_ref=psend.at[s], dst_ref=precv.at[shard], send_sem=p_ssem.at[s], recv_sem=p_rsem.at[shard],
            device_id={"cols": shard}, device_id_type=MESH).wait_recv()
        for i in range(own):
            acc[i] += precv[shard, i].astype(F32)
    for i in range(own):
        out_ref[i] = acc[i].astype(BF16)

    for s in range(1, n):
        partial(s, place(s)[2]).wait_send()
    for shard in range(n):
        for i in range(own):
            @pl.when(jnp.logical_and(shard <= c, c < n - 1))
            def _():
                hop(shard, i, True).wait_send()

            @pl.when(jnp.logical_and(shard >= c, c > 0))
            def _():
                hop(shard, i, False).wait_send()


def partner(r, k):
    bit = (r // (1 << k)) % 2
    return r + (1 - 2 * bit) * (1 << k)


def body(n, nr, sheet, w_in, w_out):
    own, rows, width = sheet.shape
    heads = w_in.shape[1]
    hdim = w_out.shape[1] // 2
    stages = nr.bit_length() - 1
    vm = pltpu.VMEM
    dma = pltpu.SemaphoreType.DMA
    w_flat = w_in.reshape(width, heads * 6 * hdim)
    wo_flat = w_out.reshape(heads * 2 * hdim, width)
    return pl.pallas_call(
        functools.partial(kernel, n, stages),
        out_shape=jax.ShapeDtypeStruct((own, rows, width), BF16),
        in_specs=[pl.BlockSpec(memory_space=pltpu.VMEM), pl.BlockSpec(memory_space=pl.ANY),
                  pl.BlockSpec(memory_space=pl.ANY)],
        out_specs=pl.BlockSpec(memory_space=pltpu.VMEM),
        scratch_shapes=[
            vm(w_flat.shape, BF16),
            vm(wo_flat.shape, BF16),
            vm((n, own, rows, width), BF16),
            vm((n, own, rows, heads * 6 * hdim), BF16),
            vm((n, own, hdim, heads * hdim), F32),
            vm((n, own, hdim, heads * hdim), F32),
            vm((n, stages, own, hdim, heads * hdim), BF16),
            vm((n, stages, own, hdim, heads * hdim), BF16),
            vm((n, own, rows, heads * 2 * hdim), BF16),
            vm((n, own, rows, width), BF16),
            vm((n, own, rows, width), BF16),
            vm((own, rows, width), F32),
            dma((2,)), dma((n, own)), dma((n, own)), dma((n, own)), dma((n, own)),
            dma((n, stages)), dma((n, stages)), dma((n,)), dma((n,)),
        ],
        compiler_params=pltpu.CompilerParams(
            collective_id=0, has_side_effects=True, vmem_limit_bytes=56 * 1024 * 1024),
    )(sheet, w_flat, wo_flat)


def solution(mesh):
    return jax.shard_map(
        functools.partial(body, mesh.shape["cols"], mesh.shape["rows"]),
        mesh=mesh,
        in_specs=(P("cols", "rows", None), P(None, "cols", None), P("cols", None, None)),
        out_specs=P("cols", "rows", None),
        check_vma=False,
    )
```

time: 233 us -> 99.5 us (0.43)
  waiting for transfers between devices: 138 us -> 0 us
  Pallas kernels: 0 us -> 93.3 us
  matrix products: 27.3 us -> 0 us
  local copies, waits for them, and re-layouts: 30.7 us -> 5.97 us
  other arithmetic: 22.4 us -> 0 us
  between operations: 13.3 us -> 0.01 us
    pallas_call x0 -> x1, Pallas kernels: none -> 93.3 us  [body(): pl.pallas_call(functools.partial(kernel, n, stages), out_shape=jax.ShapeD...]
    reduce_scatter x1 -> x0, waiting for transfers between devices: 76.9 us -> none  [body(): lax.psum_scatter(flat.reshape(lax.axis_size('cols') * own_cols, row_count...]
    all_gather x2 -> x0, waiting for transfers between devices: 60.6 us -> none  [the longest x1 41.5 us: body(): piece = lax.all_gather(sheet, 'cols', axis=0, tiled=True)]
    dot_general x8 -> x0, matrix products: 27.3 us -> none  [the longest x1 6.19 us: body(): jnp.dot(normed.reshape(-1, width), w_flat, preferred_element_type=jnp.flo...]
    select_n x8 -> x0, other arithmetic: 12.7 us -> none  [turn(): return jnp.where(reached, new, before)]
    squeeze x4 -> x0, local copies, waits for them, and re-layouts: 11 us -> none  [body(): qrow, krow, vrow = (parts[:, :, :, 0], parts[:, :, :, 1], parts[:, :, :, 2])]
    dot_general x3 -> x0, local copies, waits for them, and re-layouts: 9.52 us -> none  [the longest x1 4.64 us: body(): jnp.dot(normed.reshape(-1, width), w_flat, preferred_element_type=jnp.flo...]
    reduce_sum x3 -> x0, other arithmetic: 4.24 us -> none  [the longest x1 2.12 us: head_norm(): jnp.mean(values * values, axis=-1, keepdims=True) + 1e-06]
  transfers between devices with their start and end apart: 3 -> 0, of which waited for: 3 -> 0; matrix products, arithmetic and copies ran while one was open for 18% -> 0% of each run, Pallas kernels for 0% -> 0%
where the time goes in v1:
time: 99.5 us; the launch traced here: 99.3 us
  Pallas kernels  93.3 us (94%)
  local copies, waits for them, and re-layouts  5.97 us (6%)
    pallas_call x1, Pallas kernels, body(): pl.pallas_call(functools.partial(kernel, n, stages), out_shape=jax.ShapeD...  93.3 us
    unnamed x2, local copies, waits for them, and re-layouts  5.97 us

profile of v1, /device:TPU:0, one launch (start us, length us, event | category | flops | bytes accessed | tf_op | source)
XLA Modules:
  0.0 99.3 jit_solution(636683402353894692)
XLA Ops:
  0.0 4.1 %copy.4 = bf16[128,8,4,384]{3,1,2,0:T(8,128)(2,1)} copy(bf16[128,8,4,384]{3,2,1,0:T(4,128)(2,1)} %bitcast.4) | data formatting | bytes 6291456
  4.1 93.3 %shard_map.37 = bf16[2,128,1024]{2,1,0:T(8,128)(2,1)} custom-call(bf16[2,128,1024]{2,1,0:T(8,128)(2,1)} %x_ref.1, bf16[1024,1536]{1,0:T(8,128)(2,1)} %bitcast.3, bf16[512,1024]{1,0:T(8,128)(2,1)} %bitcast.5), custom_call_target="tpu_custom_call" | custom-call | tf_op jit(solution)/shard_map/pallas_call | solution.py:238
  97.4 1.9 %copy.6 = bf16[2,128,1024]{2,1,0:T(8,128)(2,1)} copy(bf16[2,128,1024]{2,1,0:T(8,128)(2,1)} %shard_map.37) | data formatting | bytes 1048576

commit v2 on v1

v2 whole, which is shorter than its diff:
```python
import functools

import jax
import jax.numpy as jnp
from jax import lax
from jax.experimental import pallas as pl
from jax.experimental.pallas import tpu as pltpu
from jax.sharding import PartitionSpec as P

MESH = pl.DeviceIdType.MESH
F32, BF16 = jnp.float32, jnp.bfloat16
EPS = 1e-06
GROUP = 16
PARTS = 2


def dot(a, b, dims=((1,), (0,))):
    return lax.dot_general(a, b, (dims, ((), ())), preferred_element_type=F32)


def kernel(n, stages, x_ref, w_hbm, wo_hbm, out_ref, w, w_all, buf, feat, tot, prior, st_send, st_recv, row_res,
           col_res, row_got, col_got, acc, load_sem, wo_sem, right_send, right_recv, left_send, left_recv, st_ssem,
           st_rsem, wz_ssem, wz_rsem, wb_ssem, wb_rsem, row_ssem, row_rsem, col_ssem, col_rsem):
    own, rows, width = x_ref.shape
    heads = w.shape[1] // 384
    hdim = 64
    c = lax.axis_index("cols")
    r = lax.axis_index("rows")

    w_copy = pltpu.make_async_copy(w_hbm, w, load_sem.at[0])
    w_copy.start()

    nr = w_all.shape[1]
    per = nr // (2 * heads)
    wo_copies = [
        pltpu.make_async_copy(
            wo_hbm.at[pl.ds((h * 2 + kind) * per, per)],
            w_all.at[c, pl.ds((kind * heads + h) * per, per)],
            wo_sem.at[kind, h])
        for kind in range(2) for h in range(heads)]
    for copy in wo_copies:
        copy.start()

    both = jnp.minimum(c, n - 1 - c)
    more_left = c > n - 1 - c

    def place(s):
        paired = s <= 2 * both
        dist = jnp.where(paired, (s + 1) // 2, s - both)
        is_left = jnp.where(paired, s % 2 == 1, more_left)
        return dist, is_left, jnp.where(is_left, c - dist, c + dist)

    barrier = pltpu.get_barrier_semaphore()
    for s in range(1, n):
        pl.semaphore_signal(barrier, inc=1, device_id={"cols": lax.rem(c + s, n)}, device_id_type=MESH)
    for t in range(1, nr):
        pl.semaphore_signal(barrier, inc=1, device_id={"rows": lax.rem(r + t, nr)}, device_id_type=MESH)

    for i in range(own):
        xf = x_ref[i].astype(F32)
        buf[c, i] = (xf * lax.rsqrt(jnp.mean(xf * xf, axis=-1, keepdims=True) + EPS)).astype(BF16)
    pl.semaphore_wait(barrier, n - 1 + nr - 1)

    def hop(shard, i, to_right):
        ssem, rsem = (right_send, right_recv) if to_right else (left_send, left_recv)
        to = jnp.minimum(c + 1, n - 1) if to_right else jnp.maximum(c - 1, 0)
        return pltpu.make_async_remote_copy(
            src_ref=buf.at[shard, i], dst_ref=buf.at[shard, i], send_sem=ssem.at[shard, i], recv_sem=rsem.at[shard, i],
            device_id={"cols": to}, device_id_type=MESH)

    for i in range(own):
        @pl.when(c < n - 1)
        def _():
            hop(c, i, True).start()

        @pl.when(c > 0)
        def _():
            hop(c, i, False).start()

    for copy in wo_copies:
        copy.wait()

    def give(s):
        return pltpu.make_async_remote_copy(
            src_ref=w_all.at[c, r], dst_ref=w_all.at[c, r], send_sem=wz_ssem.at[s], recv_sem=wz_rsem.at[c],
            device_id={"cols": lax.rem(c + s, n)}, device_id_type=MESH)

    def spread_out(j, t):
        return pltpu.make_async_remote_copy(
            src_ref=w_all.at[j, r], dst_ref=w_all.at[j, r], send_sem=wb_ssem.at[j, t], recv_sem=wb_rsem.at[j, r],
            device_id={"rows": lax.rem(r + t, nr)}, device_id_type=MESH)

    for s in range(1, n):
        give(s).start()

    def pass_on(j):
        pltpu.make_async_remote_copy(
            src_ref=w_all.at[j, r], dst_ref=w_all.at[j, r], send_sem=wz_ssem.at[0], recv_sem=wz_rsem.at[j],
            device_id={"cols": j}, device_id_type=MESH).wait_recv()
        for t in range(1, nr):
            spread_out(j, t).start()

    lane = lax.broadcasted_iota(jnp.int32, (1, 128), 1)
    low = lane < hdim
    spread = jnp.where(
        (lax.broadcasted_iota(jnp.int32, (128, 128), 0) < hdim) == (lax.broadcasted_iota(jnp.int32, (128, 128), 1) < hdim),
        1.0 / hdim, 0.0).astype(BF16)

    def phi(v):
        return jnp.where(v > 0, v + 1.0, jnp.exp(jnp.minimum(v, 0.0)))

    def project(s, shard, i):
        xn = buf[shard, i]
        states = []
        for h in range(heads):
            proj = dot(xn, w[:, h * 384:(h + 1) * 384])
            t0, t1, t2 = proj[:, :128], proj[:, 128:256], proj[:, 256:]
            t0 = t0 * lax.rsqrt(dot((t0 * t0).astype(BF16), spread) + EPS)
            t1 = jnp.where(low, t1, phi(t1))
            t2 = jnp.where(low, phi(t2), t2).astype(BF16)
            feat[s, i, :, h * 384:h * 384 + 128] = t0.astype(BF16)
            feat[s, i, :, h * 384 + 128:h * 384 + 256] = t1.astype(BF16)
            feat[s, i, :, h * 384 + 256:h * 384 + 384] = t2
            states.append(dot(t2, t2, ((0,), (0,)))[:hdim, hdim:])
        tot[s, i] = jnp.concatenate(states, axis=-1)

    def exchange(s, k):
        return pltpu.make_async_remote_copy(
            src_ref=st_send.at[s, k], dst_ref=st_recv.at[s, k], send_sem=st_ssem.at[s, k], recv_sem=st_rsem.at[s, k],
            device_id={"rows": partner(r, k)}, device_id_type=MESH)

    def begin(s, k):
        st_send[s, k] = tot[s].astype(BF16)
        exchange(s, k).start()

    def advance(s, k):
        exchange(s, k).wait()
        got = st_recv[s, k].astype(F32)
        later = ((r // (1 << k)) % 2).astype(F32)
        prior[s] += got * later
        if k + 1 < stages:
            tot[s] += got
            begin(s, k + 1)

    causal = lax.broadcasted_iota(jnp.int32, (rows, rows), 0) >= lax.broadcasted_iota(jnp.int32, (rows, rows), 1)

    def columns(s):
        for i in range(own):
            for h in range(heads):
                fq = feat[s, i, :, h * 384 + 128:h * 384 + 256][:, hdim:]
                t2 = feat[s, i, :, h * 384 + 256:h * 384 + 384]
                fk, vcol = t2[:, :hdim], t2[:, hdim:]
                inner = jnp.where(causal, dot(fq, fk, ((1,), (1,))), 0.0).astype(BF16)
                pre = dot(inner, vcol) + dot(fq, prior[s, i, :, h * hdim:(h + 1) * hdim].astype(BF16))
                ocol = pre * lax.rsqrt(jnp.mean(pre * pre, axis=-1, keepdims=True) + EPS)
                col_res[s, i, :, h * hdim:(h + 1) * hdim] = ocol.astype(BF16)

    def col_copy(s, slot):
        return pltpu.make_async_remote_copy(
            src_ref=col_res.at[s], dst_ref=col_got.at[slot], send_sem=col_ssem.at[s], recv_sem=col_rsem.at[slot],
            device_id={"cols": place(s)[2]}, device_id_type=MESH)

    def row_copy(s, p, slot):
        at = pl.ds(p * (rows // PARTS), rows // PARTS)
        return pltpu.make_async_remote_copy(
            src_ref=row_res.at[s, :, at], dst_ref=row_got.at[slot, :, at], send_sem=row_ssem.at[s, p],
            recv_sem=row_rsem.at[slot, p], device_id={"cols": place(s)[2]}, device_id_type=MESH)

    prior[...] = jnp.zeros_like(prior)
    pending = []

    def tick():
        for at in list(pending):
            advance(*at)
            pending.remove(at)
            if at[1] + 1 < stages:
                pending.append((at[0], at[1] + 1))
            else:
                columns(at[0])
                if at[0]:
                    col_copy(at[0], c).start()

    w_copy.wait()
    for s in range(n):
        dist, is_left, shard = place(s) if s else (0, None, c)
        for i in range(own):
            if s:
                @pl.when(is_left)
                def _():
                    hop(shard, i, True).wait_recv()

                    @pl.when(c < n - 1)
                    def _():
                        hop(shard, i, True).start()

                @pl.when(jnp.logical_not(is_left))
                def _():
                    hop(shard, i, False).wait_recv()

                    @pl.when(c > 0)
                    def _():
                        hop(shard, i, False).start()
            project(s, shard, i)
            if i == own - 1:
                begin(s, 0)
            tick()
        pending.append((s, 0))
        if s == 1:
            pass_on(place(1)[2])
        if s == 2:
            for later in range(2, n):
                pass_on(place(later)[2])

    cells = n * own * GROUP
    same = (lax.broadcasted_iota(jnp.int32, (cells, cells), 0) % GROUP) == (
        lax.broadcasted_iota(jnp.int32, (cells, cells), 1) % GROUP)

    def row_group(g, carry):
        at = pl.ds(pl.multiple_of(g * GROUP, GROUP), GROUP)
        for h in range(heads):
            t0 = feat[:, :, at, h * 384:h * 384 + 128].reshape(cells, 128)
            v = feat[:, :, at, h * 384 + 128:h * 384 + 256].reshape(cells, 128)[:, :hdim]
            score = dot(t0[:, :hdim], t0[:, hdim:], ((1,), (1,))) * (hdim ** -0.5)
            expo = jnp.where(same, jnp.exp(score), 0.0)
            weights = (expo / jnp.sum(expo, axis=-1, keepdims=True)).astype(BF16)
            orow = dot(weights, v).astype(BF16)
            row_res[:, :, at, h * hdim:(h + 1) * hdim] = orow.reshape(n, own, GROUP, hdim)
        return carry

    groups = rows // GROUP
    for p in range(PARTS):
        lax.fori_loop(groups * p // PARTS, groups * (p + 1) // PARTS, row_group, 0)
        for s in range(n - 1, 0, -1):
            row_copy(s, p, c).start()
        tick()
    while pending:
        tick()

    def combine(slot, i, row, col):
        half = nr // 2
        w_row = w_all[slot, :half].reshape(heads * hdim, width)
        w_col = w_all[slot, half:].reshape(heads * hdim, width)
        return dot(row, w_row) + dot(col, w_col)

    for i in range(own):
        acc[i] = combine(c, i, row_res[0, i], col_res[0, i])
    for s in range(1, n):
        shard = place(s)[2]
        for t in range(1, nr):
            sender = lax.rem(r + t, nr)
            pltpu.make_async_remote_copy(
                src_ref=w_all.at[shard, sender], dst_ref=w_all.at[shard, sender], send_sem=wb_ssem.at[shard, t],
                recv_sem=wb_rsem.at[shard, sender], device_id={"rows": sender}, device_id_type=MESH).wait_recv()
        for p in range(PARTS):
            row_copy(s, p, shard).wait_recv()
        col_copy(s, shard).wait_recv()
        for i in range(own):
            acc[i] += combine(shard, i, row_got[shard, i], col_got[shard, i])
    for i in range(own):
        out_ref[i] = acc[i].astype(BF16)

    for s in range(1, n):
        give(s).wait_send()
        col_copy(s, c).wait_send()
        for p in range(PARTS):
            row_copy(s, p, c).wait_send()
        for t in range(1, nr):
            spread_out(place(s)[2], t).wait_send()
    for shard in range(n):
        for i in range(own):
            @pl.when(jnp.logical_and(shard <= c, c < n - 1))
            def _():
                hop(shard, i, True).wait_send()

            @pl.when(jnp.logical_and(shard >= c, c > 0))
            def _():
                hop(shard, i, False).wait_send()


def partner(r, k):
    bit = (r // (1 << k)) % 2
    return r + (1 - 2 * bit) * (1 << k)


def body(n, nr, sheet, w_in, w_out):
    own, rows, width = sheet.shape
    heads = w_in.shape[1]
    hdim = w_out.shape[1] // 2
    stages = nr.bit_length() - 1
    vm = pltpu.VMEM
    dma = pltpu.SemaphoreType.DMA
    w_flat = w_in.reshape(width, heads * 6 * hdim)
    wo_flat = w_out.reshape(nr, heads * 2 * hdim // nr, width)
    return pl.pallas_call(
        functools.partial(kernel, n, stages),
        out_shape=jax.ShapeDtypeStruct((own, rows, width), BF16),
        in_specs=[pl.BlockSpec(memory_space=pltpu.VMEM), pl.BlockSpec(memory_space=pl.ANY),
                  pl.BlockSpec(memory_space=pl.ANY)],
        out_specs=pl.BlockSpec(memory_space=pltpu.VMEM),
        scratch_shapes=[
            vm(w_flat.shape, BF16),
            vm((n,) + wo_flat.shape, BF16),
            vm((n, own, rows, width), BF16),
            vm((n, own, rows, heads * 6 * hdim), BF16),
            vm((n, own, hdim, heads * hdim), F32),
            vm((n, own, hdim, heads * hdim), F32),
            vm((n, stages, own, hdim, heads * hdim), BF16),
            vm((n, stages, own, hdim, heads * hdim), BF16),
            vm((n, own, rows, heads * hdim), BF16),
            vm((n, own, rows, heads * hdim), BF16),
            vm((n, own, rows, heads * hdim), BF16),
            vm((n, own, rows, heads * hdim), BF16),
            vm((own, rows, width), F32),
            dma((1,)), dma((2, heads)), dma((n, own)), dma((n, own)), dma((n, own)), dma((n, own)),
            dma((n, stages)), dma((n, stages)), dma((n,)), dma((n,)), dma((n, nr)), dma((n, nr)),
            dma((n, PARTS)), dma((n, PARTS)), dma((n,)), dma((n,)),
        ],
        compiler_params=pltpu.CompilerParams(
            collective_id=0, has_side_effects=True, vmem_limit_bytes=56 * 1024 * 1024),
    )(sheet, w_flat, wo_flat)


def solution(mesh):
    return jax.shard_map(
        functools.partial(body, mesh.shape["cols"], mesh.shape["rows"]),
        mesh=mesh,
        in_specs=(P("cols", "rows", None), P(None, "cols", None), P("cols", None, None)),
        out_specs=P("cols", "rows", None),
        check_vma=False,
    )
```

time: 99.5 us -> 96.5 us (0.970)
  Pallas kernels: 93.3 us -> 90.2 us
    pallas_call x1, Pallas kernels: 93.3 us -> 90.2 us  [body(): pl.pallas_call(functools.partial(kernel, n, stages), out_shape=jax.ShapeD...]
where the time goes in v2:
time: 96.5 us; the launch traced here: 96.2 us
  Pallas kernels  90.2 us (93%)
  local copies, waits for them, and re-layouts  5.97 us (6%)
    pallas_call x1, Pallas kernels, body(): pl.pallas_call(functools.partial(kernel, n, stages), out_shape=jax.ShapeD...  90.2 us
    unnamed x2, local copies, waits for them, and re-layouts  5.97 us

profile of v2, /device:TPU:0, one launch (start us, length us, event | category | flops | bytes accessed | tf_op | source)
XLA Modules:
  0.0 96.2 jit_solution(17060368307035119138)
XLA Ops:
  0.0 4.1 %copy.4 = bf16[128,8,4,384]{3,1,2,0:T(8,128)(2,1)} copy(bf16[128,8,4,384]{3,2,1,0:T(4,128)(2,1)} %bitcast.4) | data formatting | bytes 6291456
  4.1 90.2 %shard_map.37 = bf16[2,128,1024]{2,1,0:T(8,128)(2,1)} custom-call(bf16[2,128,1024]{2,1,0:T(8,128)(2,1)} %x_ref.1, bf16[1024,1536]{1,0:T(8,128)(2,1)} %bitcast.3, bf16[8,64,1024]{2,1,0:T(8,128)(2,1)} %bitcast.5), custom_call_target="tpu_custom_call" | custom-call | tf_op jit(solution)/shard_map/pallas_call | solution.py:294
  94.4 1.9 %copy.6 = bf16[2,128,1024]{2,1,0:T(8,128)(2,1)} copy(bf16[2,128,1024]{2,1,0:T(8,128)(2,1)} %shard_map.37) | data formatting | bytes 1048576

commit v3 on v2

--- a/solution.py
+++ b/solution.py
@@ -219,11 +219,11 @@
         at = pl.ds(pl.multiple_of(g * GROUP, GROUP), GROUP)
         for h in range(heads):
             t0 = feat[:, :, at, h * 384:h * 384 + 128].reshape(cells, 128)
-            v = feat[:, :, at, h * 384 + 128:h * 384 + 256].reshape(cells, 128)[:, :hdim]
+            v = feat[:, :, at, h * 384 + 128:h * 384 + 256].reshape(cells, 128)
             score = dot(t0[:, :hdim], t0[:, hdim:], ((1,), (1,))) * (hdim ** -0.5)
-            expo = jnp.where(same, jnp.exp(score), 0.0)
-            weights = (expo / jnp.sum(expo, axis=-1, keepdims=True)).astype(BF16)
-            orow = dot(weights, v).astype(BF16)
+            expo = jnp.where(same, jnp.exp(score), 0.0).astype(BF16)
+            both_sums = dot(expo, jnp.where(low, v, jnp.ones_like(v)))
+            orow = (both_sums[:, :hdim] / both_sums[:, hdim:]).astype(BF16)
             row_res[:, :, at, h * hdim:(h + 1) * hdim] = orow.reshape(n, own, GROUP, hdim)
         return carry
 

time: 96.5 us -> 95.3 us (0.988)
  Pallas kernels: 90.2 us -> 89.1 us
    pallas_call x1, Pallas kernels: 90.2 us -> 89.1 us  [body(): pl.pallas_call(functools.partial(kernel, n, stages), out_shape=jax.ShapeD...]
where the time goes in v3:
time: 95.3 us; the launch traced here: 95 us
  Pallas kernels  89.1 us (93%)
  local copies, waits for them, and re-layouts  5.97 us (6%)
    pallas_call x1, Pallas kernels, body(): pl.pallas_call(functools.partial(kernel, n, stages), out_shape=jax.ShapeD...  89.1 us
    unnamed x2, local copies, waits for them, and re-layouts  5.97 us

profile of v3, /device:TPU:0, one launch (start us, length us, event | category | flops | bytes accessed | tf_op | source)
XLA Modules:
  0.0 95.0 jit_solution(9123060681760124553)
XLA Ops:
  0.0 4.1 %copy.4 = bf16[128,8,4,384]{3,1,2,0:T(8,128)(2,1)} copy(bf16[128,8,4,384]{3,2,1,0:T(4,128)(2,1)} %bitcast.4) | data formatting | bytes 6291456
  4.1 89.1 %shard_map.37 = bf16[2,128,1024]{2,1,0:T(8,128)(2,1)} custom-call(bf16[2,128,1024]{2,1,0:T(8,128)(2,1)} %x_ref.1, bf16[1024,1536]{1,0:T(8,128)(2,1)} %bitcast.3, bf16[8,64,1024]{2,1,0:T(8,128)(2,1)} %bitcast.5), custom_call_target="tpu_custom_call" | custom-call | tf_op jit(solution)/shard_map/pallas_call | solution.py:294
  93.2 1.9 %copy.6 = bf16[2,128,1024]{2,1,0:T(8,128)(2,1)} copy(bf16[2,128,1024]{2,1,0:T(8,128)(2,1)} %shard_map.37) | data formatting | bytes 1048576
